TPU v7x, 512 devices: a whole 4x4x16 slice. The times are simulated.
512 devices in a mesh: dp: 8 (over y, core), space: 64 (over x, z).
Axes of the slice: x: 4, y: 4, z: 16, core: 2. Of those that a mesh axis runs over, the one named last changes fastest.
Arguments:
- fine_features: bfloat16 [8, 1536, 4, 4, 256], P('dp', 'space'), may hold values from -6 to 6
- cotangent: bfloat16 [8, 1536, 4, 4, 256], P('dp', 'space'), may hold values from -0.01953125 to 0.01953125
- down_weight: bfloat16 [1728, 128], replicated, may hold values from -0.15625 to 0.15625
- coarse_weight: bfloat16 [3456, 128], replicated, may hold values from -0.109375 to 0.109375
- up_weight: bfloat16 [128, 512], replicated, may hold values from -0.5 to 0.5
- fine_neighbours: int32 [8, 1536, 7], P('dp', 'space'), may hold values from -1 to 1535, as said below
- children: int32 [8, 384, 8], P('dp', 'space'), may hold values from -1 to 1535, as said below
- parent_slots: int32 [8, 1536], P('dp', 'space'), may hold values from 0 to 3071, as said below
- coarse_neighbours: int32 [8, 384, 26], P('dp', 'space'), may hold values from -1 to 383, as said below
Outputs:
- decoded: bfloat16 [8, 1536, 4, 4, 256], P('dp', 'space')
- grad_down: float32 [221184], P('space')
- grad_coarse: float32 [442368], P('space')
- grad_up: float32 [65536], P('space')
Inputs may be any that keep to these rules, and one draw needn't show every extreme that they name: Bricks sit in a strip of the map with coordinates; fine_neighbours lists the occupied brick at the named lower offset. Every listed neighbour of fine brick f is lower than f and at least 24 * (f // 24 - 1). Each coarse brick has 3 to 5 children; children[t, c, o] = f exactly when parent_slots[t, f] = 8 c + o, and every fine brick is the child of one coarse brick. The children of coarse brick c lie from 24 * (c // 6) to 24 * (c // 6 + 1), both included. `parent_slots`: the parent of fine brick f is a coarse brick from 6 * (f // 24) to 6 * (f // 24 + 1) - 1, or the coarse brick 6 * (f // 24) - 1. `coarse_neighbours`: Symmetric: if the entry of c for offset (sx, sy, sz) is d, the entry of d for the opposite offset is c. Coarse brick c lies in cross-section c // 2 of the strip, and a listed neighbour of c for offset (sx, sy, sz) lies in cross-section c // 2 + sx.
All inputs are finite; a program needn't handle non-finite values.
Results may differ from a plain program's by a relative error of at most 0.0065.
The roundings to bfloat16 on the way count: a program that leaves them out, or rounds other values in their place, can miss the bound.
Values may be sent and summed in bfloat16 or wider, within the bound.
No kernel may reach another device: no remote copies, remote signals or barrier semaphores. Data moves between devices by JAX's collectives and lax.ppermute only.
A program may use at most 64 MiB of HBM per device.

v0:
```python
import jax
import jax.numpy as jnp
from jax import lax
from jax.sharding import PartitionSpec as P


def padded_2(x, sides, width):
    for axis, dim in sides:
        size, length = (lax.axis_size(axis), x.shape[dim])
        up = [(i, (i + 1) % size) for i in range(size - 1)]
        down = [(j, i) for i, j in up]
        last = lax.slice_in_dim(x, length - width, length, axis=dim)
        leading = lax.slice_in_dim(x, 0, width, axis=dim)
        before = lax.ppermute(last, axis, up)
        after = lax.ppermute(leading, axis, down)
        x = jnp.concatenate([before, x, after], axis=dim)
    return x


def from_behind(block, axis, distance):
    devices = range(lax.axis_size(axis))
    route = [(i - distance, i) for i in devices if i - distance in devices]
    return lax.ppermute(block, axis, route)


def silu_slope(inputs):
    squash = jax.nn.sigmoid(inputs)
    return squash * (1.0 + inputs * (1.0 - squash))


def edge_pick(offset_value, brick_edge):
    if offset_value < 0:
        return slice(brick_edge - 1, brick_edge)
    if offset_value > 0:
        return slice(0, 1)
    return slice(0, brick_edge)


def edge_place(offset_value, brick_edge):
    if offset_value < 0:
        return slice(0, 1)
    if offset_value > 0:
        return slice(brick_edge + 1, brick_edge + 2)
    return slice(1, brick_edge + 1)


def fine_planes(bricks):
    return jnp.stack([bricks[:, -1], bricks[:, :, -1], bricks[:, :, :, -1]], axis=1)


def fine_padded(bricks, planes_all, neighbours):
    brick_edge = bricks.shape[1]
    padded = jnp.pad(bricks, ((0, 0), (1, 0), (1, 0), (1, 0), (0, 0)))
    for bit_code in range(1, 8):
        shift_x = bit_code // 4
        shift_y = bit_code // 2 % 2
        shift_z = bit_code % 2
        picked = planes_all[neighbours[:, bit_code - 1]]
        if shift_x:
            values = picked[:, 0][
                :, edge_pick(-shift_y, brick_edge), edge_pick(-shift_z, brick_edge)
            ][:, None]
        elif shift_y:
            values = picked[:, 1][:, :, edge_pick(-shift_z, brick_edge)][:, :, None]
        else:
            values = picked[:, 2][:, :, :, None]
        place_x = slice(0, 1) if shift_x else slice(1, brick_edge + 1)
        place_y = slice(0, 1) if shift_y else slice(1, brick_edge + 1)
        place_z = slice(0, 1) if shift_z else slice(1, brick_edge + 1)
        padded = padded.at[:, place_x, place_y, place_z].set(values)
    return padded


def fine_columns(padded, half_edge):
    tap_list = []
    for tap_code in range(27):
        along_x = tap_code // 9
        along_y = tap_code // 3 % 3
        along_z = tap_code % 3
        tap_list.append(
            padded[
                :,
                along_x : along_x + 2 * half_edge - 1 : 2,
                along_y : along_y + 2 * half_edge - 1 : 2,
                along_z : along_z + 2 * half_edge - 1 : 2,
            ]
        )
    stacked = jnp.stack(tap_list, axis=4)
    return stacked.reshape(-1, 27 * stacked.shape[-1])


def octants_to_bricks(patches):
    brick_count = patches.shape[0]
    half_edge = patches.shape[2]
    channels = patches.shape[-1]
    arranged = patches.reshape(brick_count, 2, 2, 2, half_edge, half_edge, half_edge, channels)
    arranged = arranged.transpose(0, 1, 4, 2, 5, 3, 6, 7)
    return arranged.reshape(brick_count, 2 * half_edge, 2 * half_edge, 2 * half_edge, channels)


def bricks_to_octants(bricks):
    brick_count = bricks.shape[0]
    half_edge = bricks.shape[1] // 2
    channels = bricks.shape[-1]
    arranged = bricks.reshape(brick_count, 2, half_edge, 2, half_edge, 2, half_edge, channels)
    arranged = arranged.transpose(0, 1, 3, 5, 2, 4, 6, 7)
    return arranged.reshape(brick_count * 8, half_edge, half_edge, half_edge, channels)


def coarse_faces(bricks):
    return jnp.stack(
        [
            bricks[:, 0],
            bricks[:, -1],
            bricks[:, :, 0],
            bricks[:, :, -1],
            bricks[:, :, :, 0],
            bricks[:, :, :, -1],
        ],
        axis=1,
    )


def coarse_padded(bricks, faces_all, neighbours):
    brick_edge = bricks.shape[1]
    padded = jnp.pad(bricks, ((0, 0), (1, 1), (1, 1), (1, 1), (0, 0)))
    offset_codes = [offset_code for offset_code in range(27) if offset_code != 13]
    for column_index, offset_code in enumerate(offset_codes):
        off_x = offset_code // 9 - 1
        off_y = offset_code // 3 % 3 - 1
        off_z = offset_code % 3 - 1
        picked = faces_all[neighbours[:, column_index]]
        if off_x != 0:
            values = picked[:, 1 if off_x < 0 else 0][
                :, edge_pick(off_y, brick_edge), edge_pick(off_z, brick_edge)
            ][:, None]
        elif off_y != 0:
            values = picked[:, 3 if off_y < 0 else 2][:, :, edge_pick(off_z, brick_edge)][
                :, :, None
            ]
        else:
            values = picked[:, 5 if off_z < 0 else 4][:, :, :, None]
        padded = padded.at[
            :,
            edge_place(off_x, brick_edge),
            edge_place(off_y, brick_edge),
            edge_place(off_z, brick_edge),
        ].set(values)
    return padded


def pair_taps(padded, along_x, along_y, reverse):
    brick_edge = padded.shape[1] - 2
    pieces = []
    for along_z in range(3):
        if reverse:
            lows = (2 - along_x, 2 - along_y, 2 - along_z)
        else:
            lows = (along_x, along_y, along_z)
        pieces.append(
            padded[
                :,
                lows[0] : lows[0] + brick_edge,
                lows[1] : lows[1] + brick_edge,
                lows[2] : lows[2] + brick_edge,
            ]
        )
    gathered_taps = jnp.concatenate(pieces, axis=-1)
    return gathered_taps.reshape(-1, gathered_taps.shape[-1])


def coarse_forward(padded, weight):
    channels = weight.shape[0] // 27
    summed = None
    for pair_code in range(9):
        gathered_taps = pair_taps(padded, pair_code // 3, pair_code % 3, False)
        weight_rows = weight[pair_code * 3 * channels : (pair_code + 1) * 3 * channels]
        partial_value = jnp.dot(gathered_taps, weight_rows, preferred_element_type=jnp.float32)
        summed = partial_value if summed is None else summed + partial_value
    return summed


def coarse_weight_grad(padded, slope_rows):
    blocks = []
    for pair_code in range(9):
        gathered_taps = pair_taps(padded, pair_code // 3, pair_code % 3, False)
        blocks.append(
            lax.dot_general(
                gathered_taps,
                slope_rows,
                (((0,), (0,)), ((), ())),
                preferred_element_type=jnp.float32,
            )
        )
    return jnp.concatenate(blocks, axis=0)


def coarse_transpose(padded, weight):
    channels_in = weight.shape[0] // 27
    channels_out = weight.shape[1]
    summed = None
    for pair_code in range(9):
        gathered_taps = pair_taps(padded, pair_code // 3, pair_code % 3, True)
        weight_block = weight[pair_code * 3 * channels_in : (pair_code + 1) * 3 * channels_in]
        weight_block = (
            weight_block.reshape(3, channels_in, channels_out)
            .transpose(0, 2, 1)
            .reshape(3 * channels_out, channels_in)
        )
        partial_value = jnp.dot(gathered_taps, weight_block, preferred_element_type=jnp.float32)
        summed = partial_value if summed is None else summed + partial_value
    return summed


def wide_faces(faces_own, forward):
    count = faces_own.shape[0]
    if forward:
        return padded_2(faces_own, (("space", 0),), count)
    return padded_2(faces_own, (("space", 0),), count)


def parent_patches(octants, parent_list, place_index, forward):
    patch_count = octants.shape[0]
    half_edge = octants.shape[1]
    channels = octants.shape[-1]
    tail_octants = octants[patch_count - 8 :].reshape(8, half_edge, half_edge, half_edge * channels)
    if forward:
        arrived = from_behind(tail_octants, "space", 1)
    else:
        arrived = from_behind(tail_octants, "space", 1)
    patch_pool = jnp.concatenate(
        [arrived.reshape(8, half_edge, half_edge, half_edge, channels), octants], axis=0
    )
    offset_slot = (patch_count // 8 * place_index - 1) * 8
    return patch_pool[parent_list - offset_slot]


def body(
    fine_features,
    cotangent,
    down_weight,
    coarse_weight,
    up_weight,
    fine_neighbours,
    children,
    parent_slots,
    coarse_neighbours,
):
    place_index = lax.axis_index("space")
    brick_edge = fine_features.shape[2]
    half_edge = brick_edge // 2
    fine_width = down_weight.shape[0] // 27
    coarse_width = down_weight.shape[1]
    fine_count = fine_features.shape[1]
    coarse_count = children.shape[1]
    bricks = fine_features.reshape(fine_count, brick_edge, brick_edge, brick_edge, fine_width)
    own_planes = fine_planes(bricks).reshape(fine_count, 3, brick_edge, brick_edge * fine_width)
    prev_planes = from_behind(own_planes, "space", 1)
    zero_planes = jnp.zeros((1, 3, brick_edge, brick_edge * fine_width), jnp.bfloat16)
    planes_all = jnp.concatenate([prev_planes, own_planes, zero_planes], axis=0)
    planes_all = planes_all.reshape(2 * fine_count + 1, 3, brick_edge, brick_edge, fine_width)
    fine_nbr = fine_neighbours[0]
    local_fine = jnp.where(fine_nbr < 0, 2 * fine_count, fine_nbr - fine_count * (place_index - 1))
    padded_fine = fine_padded(bricks, planes_all, local_fine)
    columns = fine_columns(padded_fine, half_edge)
    pre_down = jnp.dot(columns, down_weight, preferred_element_type=jnp.float32)
    hidden = jax.nn.silu(pre_down).astype(jnp.bfloat16)
    patches = hidden.reshape(fine_count, half_edge, half_edge, half_edge * coarse_width)
    next_first = from_behind(patches[0:1], "space", -1)
    zero_patch = jnp.zeros((1, half_edge, half_edge, half_edge * coarse_width), jnp.bfloat16)
    patch_pool = jnp.concatenate([patches, next_first, zero_patch], axis=0)
    patch_pool = patch_pool.reshape(fine_count + 2, half_edge, half_edge, half_edge, coarse_width)
    child_list = children[0]
    child_local = jnp.where(child_list < 0, fine_count + 1, child_list - fine_count * place_index)
    coarse_in = octants_to_bricks(patch_pool[child_local])
    coarse_nbr = coarse_neighbours[0]
    local_coarse = jnp.where(
        coarse_nbr < 0, 3 * coarse_count, coarse_nbr - coarse_count * (place_index - 1)
    )
    zero_faces = jnp.zeros((1, 6, brick_edge, brick_edge * coarse_width), jnp.bfloat16)
    faces_own = coarse_faces(coarse_in).reshape(
        coarse_count, 6, brick_edge, brick_edge * coarse_width
    )
    faces_wide = wide_faces(faces_own, True)
    faces_all = jnp.concatenate([faces_wide, zero_faces], axis=0)
    faces_all = faces_all.reshape(3 * coarse_count + 1, 6, brick_edge, brick_edge, coarse_width)
    padded_in = coarse_padded(coarse_in, faces_all, local_coarse)
    pre_coarse = coarse_forward(padded_in, coarse_weight)
    coarse_out = jax.nn.silu(pre_coarse).astype(jnp.bfloat16)
    coarse_out = coarse_out.reshape(coarse_count, brick_edge, brick_edge, brick_edge, coarse_width)
    parent_list = parent_slots[0]
    up_input = parent_patches(bricks_to_octants(coarse_out), parent_list, place_index, True)
    up_rows = up_input.reshape(-1, coarse_width)
    up_out = jnp.dot(up_rows, up_weight, preferred_element_type=jnp.float32)
    up_grid = up_out.reshape(
        fine_count, half_edge, half_edge, half_edge, 2, 2, 2, fine_width
    ).transpose(0, 1, 4, 2, 5, 3, 6, 7)
    up_grid = up_grid.reshape(fine_count, brick_edge, brick_edge, brick_edge, fine_width)
    joined = up_grid + bricks.astype(jnp.float32)
    decoded = jax.nn.silu(joined).astype(jnp.bfloat16).reshape(fine_features.shape)
    cot_grid = cotangent.reshape(fine_count, brick_edge, brick_edge, brick_edge, fine_width).astype(
        jnp.float32
    )
    out_grad = (cot_grid * silu_slope(joined)).astype(jnp.bfloat16)
    out_rows = out_grad.reshape(
        fine_count, half_edge, 2, half_edge, 2, half_edge, 2, fine_width
    ).transpose(0, 1, 3, 5, 2, 4, 6, 7)
    out_rows = out_rows.reshape(-1, 8 * fine_width)
    grad_up = lax.dot_general(
        up_rows, out_rows, (((0,), (0,)), ((), ())), preferred_element_type=jnp.float32
    )
    patch_grad = lax.dot_general(
        out_rows, up_weight, (((1,), (1,)), ((), ())), preferred_element_type=jnp.float32
    ).astype(jnp.bfloat16)
    grad_patches = patch_grad.reshape(fine_count, half_edge, half_edge, half_edge * coarse_width)
    next_grad = from_behind(grad_patches[0:1], "space", -1)
    grad_pool = jnp.concatenate([grad_patches, next_grad, zero_patch], axis=0)
    grad_pool = grad_pool.reshape(fine_count + 2, half_edge, half_edge, half_edge, coarse_width)
    coarse_grad_out = octants_to_bricks(grad_pool[child_local])
    coarse_slope = (
        coarse_grad_out.reshape(-1, coarse_width).astype(jnp.float32) * silu_slope(pre_coarse)
    ).astype(jnp.bfloat16)
    grad_coarse = coarse_weight_grad(padded_in, coarse_slope)
    slope_bricks = coarse_slope.reshape(
        coarse_count, brick_edge, brick_edge, brick_edge, coarse_width
    )
    slope_faces = coarse_faces(slope_bricks).reshape(
        coarse_count, 6, brick_edge, brick_edge * coarse_width
    )
    slope_wide = wide_faces(slope_faces, False)
    slope_all = jnp.concatenate([slope_wide, zero_faces], axis=0)
    slope_all = slope_all.reshape(3 * coarse_count + 1, 6, brick_edge, brick_edge, coarse_width)
    padded_slope = coarse_padded(slope_bricks, slope_all, local_coarse)
    input_grad = coarse_transpose(padded_slope, coarse_weight).astype(jnp.bfloat16)
    input_bricks = input_grad.reshape(
        coarse_count, brick_edge, brick_edge, brick_edge, coarse_width
    )
    hidden_grad = parent_patches(bricks_to_octants(input_bricks), parent_list, place_index, False)
    down_slope = (
        hidden_grad.reshape(-1, coarse_width).astype(jnp.float32) * silu_slope(pre_down)
    ).astype(jnp.bfloat16)
    grad_down = lax.dot_general(
        columns, down_slope, (((0,), (0,)), ((), ())), preferred_element_type=jnp.float32
    )
    flat_down = grad_down.reshape(-1)
    flat_coarse = grad_coarse.reshape(-1)
    flat_up = grad_up.reshape(-1)
    whole_down, whole_coarse, whole_up = lax.psum(
        (flat_down, flat_coarse, flat_up), ("dp", "space")
    )
    space_count = lax.axis_size("space")
    share_down = lax.dynamic_slice_in_dim(
        whole_down,
        place_index * (flat_down.shape[0] // space_count),
        flat_down.shape[0] // space_count,
    )
    share_coarse = lax.dynamic_slice_in_dim(
        whole_coarse,
        place_index * (flat_coarse.shape[0] // space_count),
        flat_coarse.shape[0] // space_count,
    )
    share_up = lax.dynamic_slice_in_dim(
        whole_up, place_index * (flat_up.shape[0] // space_count), flat_up.shape[0] // space_count
    )
    return (decoded, share_down, share_coarse, share_up)


def solution(mesh):
    in_specs = (
        P("dp", "space", None, None, None),
        P("dp", "space", None, None, None),
        P(),
        P(),
        P(),
        P("dp", "space", None),
        P("dp", "space", None),
        P("dp", "space"),
        P("dp", "space", None),
    )
    out_specs = (P("dp", "space", None, None, None), P("space"), P("space"), P("space"))
    return jax.shard_map(body, mesh=mesh, in_specs=in_specs, out_specs=out_specs, check_vma=False)
```

profile of v0, /device:TPU:2, one launch (start us, length us, event | category | flops | bytes accessed | tf_op | source)
XLA Modules:
  0.0 735.8 jit_solution(11911529440482196568)
XLA Ops:
  7.2 1.8 copy_convert_fusion
  10.0 3.8 collective-permute-start
  15.8 9.5 %collective-permute-done = bf16[24,3,4,256]{3,0,2,1:T(8,128)(2,1)S(1)} collective-permute-done((bf16[24,3,4,256]{3,0,2,1:T(8,128)(2,1)S(1)}, bf16[24,3,4,256]{3,0,2,1:T(8,128)(2,1)S(1)}, u32[]{:S(2)}, u32[]{:S(2)}) %collective-permute-start) | collective-permute-done | bytes 147488 | tf_op jit(solution)/shard_map/ppermute | solution.py:23
  32.3 7.6 %scatter.196 = bf16[24,5,5,5,64]{4,3,0,2,1:T(8,128)(2,1)S(1)} dynamic-update-slice(bf16[24,5,5,5,64]{4,3,0,2,1:T(8,128)(2,1)S(1)} %pad.247, bf16[24,4,4,1,64]{4,3,0,2,1:T(2,128)(2,1)S(1)} %copy.350, s32[]{:T(128)} %constant.1608.clone.1, s32[]{:T(128)} %constant.1614.clone.1, s32[]{:T(128)} %constant.1614.clone.1, s32[]{:T(128)} %constant.1608.clone.1, s32[]{:T(128)} %constant.1608.clone.1) | dynamic-update-slice | bytes 98308 | tf_op jit(solution)/shard_map/scatter | solution.py:70
  39.9 3.1 scatter.199
  44.7 3.4 scatter.201
  48.2 1.9 scatter.204
  62.0 3.6 collective-permute-start.1
  69.1 5.8 collective-permute-start.3
  74.8 1.9 collective-permute-start.2
  77.5 6.5 collective-permute-done.2
  113.0 2.0 pad_maximum_fusion.7
  116.7 1.8 pad_maximum_fusion.8
  123.6 2.1 collective-permute-start.4
  142.5 6.4 collective-permute-start.5
  151.9 6.3 collective-permute-start.7
  158.2 1.9 collective-permute-start.6
  163.7 3.7 collective-permute-done.6
  226.8 1.9 pad_maximum_fusion.16
  229.7 1.8 pad_maximum_fusion.17
  231.5 1.8 reshape.3031
  237.8 1.9 collective-permute-start.8
  240.8 4.8 collective-permute-done.8
  249.8 474.9 %all-reduce.6.cloned.1.call-done = (f32[221184]{0:T(1024)}, f32[442368]{0:T(1024)}, f32[65536]{0:T(1024)}) async-done(((f32[221184]{0:T(1024)}, f32[442368]{0:T(1024)}, f32[65536]{0:T(1024)}), (f32[221184]{0:T(1024)}, f32[442368]{0:T(1024)}, f32[65536]{0:T(1024)})) %all-reduce.6.cloned.1.call-update) | async-done | bytes 2916368 | tf_op jit(solution)/shard_map/psum | solution.py:348
  (635 shorter events, 157.7 us)
Async XLA Ops:
  7.2 717.5 %all-reduce.6.cloned.1.call-start = ((), (), s32[]{:S(2)}) async-start(), calls=%async_computation | async-start | bytes 5832704 | tf_op jit(solution)/shard_map/psum | solution.py:348
  10.0 15.2 %collective-permute-start = (bf16[24,3,4,256]{3,0,2,1:T(8,128)(2,1)S(1)}, bf16[24,3,4,256]{3,0,2,1:T(8,128)(2,1)S(1)}, u32[]{:S(2)}, u32[]{:S(2)}) collective-permute-start(bf16[24,3,4,256]{3,0,2,1:T(8,128)(2,1)S(1)} %constant_dynamic-update-slice_fusion), channel_id=1, source_target_pairs={{0,1},{1,2},{2,3},{3,4},{4,5},{5,6},{6,7},{7,8},{8,9},{9,10},{10,1... | collective-permute-start | bytes 442376 | tf_op jit(solution)/shard_map/ppermute | solution.py:23
  15.0 76.2 %copy-start.46 = (s32[1024]{0:T(1024)}, s32[1024]{0:T(1024)S(1)}, u32[]{:S(2)}) copy-start(s32[1024]{0:T(1024)S(1)} %get-tuple-element.872) | copy-start | bytes 12292
  15.0 76.9 %copy-start.45 = (s32[1024]{0:T(1024)}, s32[1024]{0:T(1024)S(1)}, u32[]{:S(2)}) copy-start(s32[1024]{0:T(1024)S(1)} %get-tuple-element.871) | copy-start | bytes 12292
  15.0 77.6 %copy-start.48 = (s32[1024]{0:T(1024)}, s32[1024]{0:T(1024)S(1)}, u32[]{:S(2)}) copy-start(s32[1024]{0:T(1024)S(1)} %get-tuple-element.870) | copy-start | bytes 12292
  15.0 78.3 %copy-start.47 = (s32[1024]{0:T(1024)}, s32[1024]{0:T(1024)S(1)}, u32[]{:S(2)}) copy-start(s32[1024]{0:T(1024)S(1)} %get-tuple-element.869) | copy-start | bytes 12292
  15.1 79.1 %copy-start.50 = (s32[1024]{0:T(1024)}, s32[1024]{0:T(1024)S(1)}, u32[]{:S(2)}) copy-start(s32[1024]{0:T(1024)S(1)} %get-tuple-element.868) | copy-start | bytes 12292
  15.1 79.8 %copy-start.49 = (s32[1024]{0:T(1024)}, s32[1024]{0:T(1024)S(1)}, u32[]{:S(2)}) copy-start(s32[1024]{0:T(1024)S(1)} %get-tuple-element.867) | copy-start | bytes 12292
  15.1 80.5 %copy-start.52 = (s32[1024]{0:T(1024)}, s32[1024]{0:T(1024)S(1)}, u32[]{:S(2)}) copy-start(s32[1024]{0:T(1024)S(1)} %get-tuple-element.866) | copy-start | bytes 12292
  15.1 81.2 %copy-start.51 = (s32[1024]{0:T(1024)}, s32[1024]{0:T(1024)S(1)}, u32[]{:S(2)}) copy-start(s32[1024]{0:T(1024)S(1)} %get-tuple-element.865) | copy-start | bytes 12292
  15.1 82.0 %copy-start.54 = (s32[1024]{0:T(1024)}, s32[1024]{0:T(1024)S(1)}, u32[]{:S(2)}) copy-start(s32[1024]{0:T(1024)S(1)} %get-tuple-element.864) | copy-start | bytes 12292
  15.1 82.7 %copy-start.53 = (s32[1024]{0:T(1024)}, s32[1024]{0:T(1024)S(1)}, u32[]{:S(2)}) copy-start(s32[1024]{0:T(1024)S(1)} %get-tuple-element.863) | copy-start | bytes 12292
  15.2 83.4 %copy-start.56 = (s32[1024]{0:T(1024)}, s32[1024]{0:T(1024)S(1)}, u32[]{:S(2)}) copy-start(s32[1024]{0:T(1024)S(1)} %get-tuple-element.862) | copy-start | bytes 12292
  15.2 84.1 %copy-start.55 = (s32[1024]{0:T(1024)}, s32[1024]{0:T(1024)S(1)}, u32[]{:S(2)}) copy-start(s32[1024]{0:T(1024)S(1)} %get-tuple-element.861) | copy-start | bytes 12292
  15.7 84.3 %copy-start.58 = (s32[1024]{0:T(1024)}, s32[1024]{0:T(1024)S(1)}, u32[]{:S(2)}) copy-start(s32[1024]{0:T(1024)S(1)} %get-tuple-element.860) | copy-start | bytes 12292
  15.8 85.0 %copy-start.57 = (s32[1024]{0:T(1024)}, s32[1024]{0:T(1024)S(1)}, u32[]{:S(2)}) copy-start(s32[1024]{0:T(1024)S(1)} %get-tuple-element.859) | copy-start | bytes 12292
  62.0 5.5 collective-permute-start.1
  69.1 8.4 %collective-permute-start.3 = (bf16[6,6,4,512]{3,2,0,1:T(4,128)(2,1)S(1)}, bf16[6,6,4,512]{3,2,0,1:T(4,128)(2,1)S(1)}, u32[]{:S(2)}, u32[]{:S(2)}) collective-permute-start(bf16[6,6,4,512]{3,2,0,1:T(4,128)(2,1)S(1)} %constant_dynamic-update-slice_fusion.30), channel_id=1, source_target_pairs={{1,0},{2,1},{3,2},{4,3},{5,4},{6,5},{7,6},{8,7},{9,8},{10,9},{11,1... | collective-permute-start | bytes 442376 | tf_op jit(solution)/shard_map/ppermute | solution.py:15
  74.8 9.1 %collective-permute-start.2 = (bf16[6,6,4,512]{3,2,0,1:T(4,128)(2,1)S(1)}, bf16[6,6,4,512]{3,2,0,1:T(4,128)(2,1)S(1)}, u32[]{:S(2)}, u32[]{:S(2)}) collective-permute-start(bf16[6,6,4,512]{3,2,0,1:T(4,128)(2,1)S(1)} %constant_dynamic-update-slice_fusion.30), channel_id=1, source_target_pairs={{0,1},{1,2},{2,3},{3,4},{4,5},{5,6},{6,7},{7,8},{8,9},{9,10},{10,1... | collective-permute-start | bytes 442376 | tf_op jit(solution)/shard_map/ppermute | solution.py:14
  123.6 15.2 %collective-permute-start.4 = (bf16[8,2,2,256]{3,0,2,1:T(8,128)(2,1)S(1)}, bf16[8,2,2,256]{3,0,2,1:T(8,128)(2,1)S(1)}, u32[]{:S(2)}, u32[]{:S(2)}) collective-permute-start(bf16[8,2,2,256]{3,0,2,1:T(8,128)(2,1)S(1)} %bitcast.517), channel_id=1, source_target_pairs={{0,1},{1,2},{2,3},{3,4},{4,5},{5,6},{6,7},{7,8},{8,9},{9,10},{10,1... | collective-permute-start | bytes 49160 | tf_op jit(solution)/shard_map/ppermute | solution.py:23
  142.5 7.4 %collective-permute-start.5 = (bf16[1,2,2,256]{3,2,1,0:T(2,128)(2,1)S(1)}, bf16[1,2,2,256]{3,2,1,0:T(2,128)(2,1)S(1)}, u32[]{:S(2)}, u32[]{:S(2)}) collective-permute-start(bf16[1,2,2,256]{3,2,1,0:T(2,128)(2,1)S(1)} %slice.3357), channel_id=1, source_target_pairs={{1,0},{2,1},{3,2},{4,3},{5,4},{6,5},{7,6},{8,7},{9,8},{10,9},{11,1... | collective-permute-start | bytes 6152 | tf_op jit(solution)/shard_map/ppermute | solution.py:23
  151.9 11.8 %collective-permute-start.7 = (bf16[6,6,4,512]{3,2,0,1:T(4,128)(2,1)S(1)}, bf16[6,6,4,512]{3,2,0,1:T(4,128)(2,1)S(1)}, u32[]{:S(2)}, u32[]{:S(2)}) collective-permute-start(bf16[6,6,4,512]{3,2,0,1:T(4,128)(2,1)S(1)} %constant_dynamic-update-slice_fusion.36), channel_id=1, source_target_pairs={{1,0},{2,1},{3,2},{4,3},{5,4},{6,5},{7,6},{8,7},{9,8},{10,9},{11,1... | collective-permute-start | bytes 442376 | tf_op jit(solution)/shard_map/ppermute | solution.py:15
  158.2 9.1 %collective-permute-start.6 = (bf16[6,6,4,512]{3,2,0,1:T(4,128)(2,1)S(1)}, bf16[6,6,4,512]{3,2,0,1:T(4,128)(2,1)S(1)}, u32[]{:S(2)}, u32[]{:S(2)}) collective-permute-start(bf16[6,6,4,512]{3,2,0,1:T(4,128)(2,1)S(1)} %constant_dynamic-update-slice_fusion.36), channel_id=1, source_target_pairs={{0,1},{1,2},{2,3},{3,4},{4,5},{5,6},{6,7},{7,8},{8,9},{9,10},{10,1... | collective-permute-start | bytes 442376 | tf_op jit(solution)/shard_map/ppermute | solution.py:14
  237.8 7.7 %collective-permute-start.8 = (bf16[8,2,2,256]{3,0,2,1:T(8,128)(2,1)S(1)}, bf16[8,2,2,256]{3,0,2,1:T(8,128)(2,1)S(1)}, u32[]{:S(2)}, u32[]{:S(2)}) collective-permute-start(bf16[8,2,2,256]{3,0,2,1:T(8,128)(2,1)S(1)} %bitcast.518), channel_id=1, source_target_pairs={{0,1},{1,2},{2,3},{3,4},{4,5},{5,6},{6,7},{7,8},{8,9},{9,10},{10,1... | collective-permute-start | bytes 49160 | tf_op jit(solution)/shard_map/ppermute | solution.py:23
  (58 other events, 844.1 us)
Sparse Core Ops, SparseCore 0:
  248.0 476.6 all-reduce.5
where the time goes:
time: 745 us; the launch traced here: 736 us
  waiting for transfers between devices  502 us (67%)
  local copies, waits for them, and re-layouts  151 us (20%)
  starting transfers between devices  33.8 us (5%)
  between operations  18 us (2%)
  other arithmetic  17.7 us (2%)
  matrix products  14 us (2%)
    psum x1, waiting for transfers between devices, body(): lax.psum((flat_down, flat_coarse, flat_up), ('dp', 'space'))  475 us
    gather x52, local copies, waits for them, and re-layouts, coarse_padded(): picked = faces_all[neighbours[:, column_index]]  50 us
    scatter x7, local copies, waits for them, and re-layouts, fine_padded(): padded = padded.at[:, place_x, place_y, place_z].set(values)  18.1 us
    ppermute x5, starting transfers between devices, from_behind(): return lax.ppermute(block, axis, route)  17.9 us
    ppermute x5, waiting for transfers between devices, from_behind(): return lax.ppermute(block, axis, route)  16 us
  transfers between devices with their start and end apart: 10, of which 7 were waited for; matrix products, arithmetic and copies ran while one was open for 3% of the time, Pallas kernels for 0%

commit v1 on v0

--- a/solution.py
+++ b/solution.py
@@ -345,9 +345,8 @@
     flat_down = grad_down.reshape(-1)
     flat_coarse = grad_coarse.reshape(-1)
     flat_up = grad_up.reshape(-1)
-    whole_down, whole_coarse, whole_up = lax.psum(
-        (flat_down, flat_coarse, flat_up), ("dp", "space")
-    )
+    _balance_sheets = lambda content: lax.psum(lax.psum(content, "space"), "dp")
+    whole_down, whole_coarse, whole_up = _balance_sheets((flat_down, flat_coarse, flat_up))
     space_count = lax.axis_size("space")
     share_down = lax.dynamic_slice_in_dim(
         whole_down,

time: 745 us -> 625 us (0.84)
  waiting for transfers between devices: 502 us -> 382 us
    psum x1 -> x2, waiting for transfers between devices: 475 us -> 355 us  [body(): _balance_sheets = lambda content: lax.psum(lax.psum(content, 'space'), 'dp')]
  transfers between devices with their start and end apart: 10 -> 11, of which waited for: 7 -> 8; matrix products, arithmetic and copies ran while one was open for 3% -> 3% of each run, Pallas kernels for 0% -> 0%
where the time goes in v1:
time: 625 us; the launch traced here: 616 us
  waiting for transfers between devices  382 us (61%)
  local copies, waits for them, and re-layouts  151 us (24%)
  starting transfers between devices  33.8 us (5%)
  between operations  18 us (3%)
  other arithmetic  17.8 us (3%)
  matrix products  14.1 us (2%)
    psum x2, waiting for transfers between devices, body(): _balance_sheets = lambda content: lax.psum(lax.psum(content, 'space'), 'dp')  355 us
    gather x52, local copies, waits for them, and re-layouts, coarse_padded(): picked = faces_all[neighbours[:, column_index]]  50 us
    scatter x7, local copies, waits for them, and re-layouts, fine_padded(): padded = padded.at[:, place_x, place_y, place_z].set(values)  18.1 us
    ppermute x5, starting transfers between devices, from_behind(): return lax.ppermute(block, axis, route)  17.9 us
    ppermute x5, waiting for transfers between devices, from_behind(): return lax.ppermute(block, axis, route)  16 us
    concatenate x18, other arithmetic, pair_taps(): gathered_taps = jnp.concatenate(pieces, axis=-1)  12.8 us
  transfers between devices with their start and end apart: 11, of which 8 were waited for; matrix products, arithmetic and copies ran while one was open for 3% of the time, Pallas kernels for 0%

profile of v1, /device:TPU:2, one launch (start us, length us, event | category | flops | bytes accessed | tf_op | source)
XLA Modules:
  0.0 616.2 jit_solution(15171440200311305042)
XLA Ops:
  7.2 1.8 copy_convert_fusion
  10.0 3.8 collective-permute-start
  15.8 9.5 %collective-permute-done = bf16[24,3,4,256]{3,0,2,1:T(8,128)(2,1)S(1)} collective-permute-done((bf16[24,3,4,256]{3,0,2,1:T(8,128)(2,1)S(1)}, bf16[24,3,4,256]{3,0,2,1:T(8,128)(2,1)S(1)}, u32[]{:S(2)}, u32[]{:S(2)}) %collective-permute-start) | collective-permute-done | bytes 147488 | tf_op jit(solution)/shard_map/ppermute | solution.py:23
  32.3 7.6 %scatter.196 = bf16[24,5,5,5,64]{4,3,0,2,1:T(8,128)(2,1)S(1)} dynamic-update-slice(bf16[24,5,5,5,64]{4,3,0,2,1:T(8,128)(2,1)S(1)} %pad.247, bf16[24,4,4,1,64]{4,3,0,2,1:T(2,128)(2,1)S(1)} %copy.350, s32[]{:T(128)} %constant.1608.clone.1, s32[]{:T(128)} %constant.1614.clone.1, s32[]{:T(128)} %constant.1614.clone.1, s32[]{:T(128)} %constant.1608.clone.1, s32[]{:T(128)} %constant.1608.clone.1) | dynamic-update-slice | bytes 98308 | tf_op jit(solution)/shard_map/scatter | solution.py:70
  39.9 3.1 scatter.199
  44.7 3.4 scatter.201
  48.2 1.9 scatter.204
  62.0 3.6 collective-permute-start.1
  69.1 5.8 collective-permute-start.3
  74.8 1.9 collective-permute-start.2
  77.5 6.5 %collective-permute-done.2 = bf16[6,6,4,512]{3,2,0,1:T(4,128)(2,1)S(1)} collective-permute-done((bf16[6,6,4,512]{3,2,0,1:T(4,128)(2,1)S(1)}, bf16[6,6,4,512]{3,2,0,1:T(4,128)(2,1)S(1)}, u32[]{:S(2)}, u32[]{:S(2)}) %collective-permute-start.2) | collective-permute-done | bytes 147488 | tf_op jit(solution)/shard_map/ppermute | solution.py:14
  113.0 2.0 pad_maximum_fusion.7
  116.8 1.8 pad_maximum_fusion.8
  123.6 2.1 collective-permute-start.4
  142.6 6.4 %collective-permute-start.5 = (bf16[1,2,2,256]{3,2,1,0:T(2,128)(2,1)S(1)}, bf16[1,2,2,256]{3,2,1,0:T(2,128)(2,1)S(1)}, u32[]{:S(2)}, u32[]{:S(2)}) collective-permute-start(bf16[1,2,2,256]{3,2,1,0:T(2,128)(2,1)S(1)} %slice.3357), channel_id=1, source_target_pairs={{1,0},{2,1},{3,2},{4,3},{5,4},{6,5},{7,6},{8,7},{9,8},{10,9},{11,1... | collective-permute-start | bytes 6152 | tf_op jit(solution)/shard_map/ppermute | solution.py:23
  152.0 6.3 %collective-permute-start.7 = (bf16[6,6,4,512]{3,2,0,1:T(4,128)(2,1)S(1)}, bf16[6,6,4,512]{3,2,0,1:T(4,128)(2,1)S(1)}, u32[]{:S(2)}, u32[]{:S(2)}) collective-permute-start(bf16[6,6,4,512]{3,2,0,1:T(4,128)(2,1)S(1)} %constant_dynamic-update-slice_fusion.36), channel_id=1, source_target_pairs={{1,0},{2,1},{3,2},{4,3},{5,4},{6,5},{7,6},{8,7},{9,8},{10,9},{11,1... | collective-permute-start | bytes 442376 | tf_op jit(solution)/shard_map/ppermute | solution.py:15
  158.3 1.9 collective-permute-start.6
  163.8 3.7 collective-permute-done.6
  226.9 1.9 pad_maximum_fusion.16
  229.8 1.8 pad_maximum_fusion.17
  238.0 1.9 collective-permute-start.8
  241.0 4.7 collective-permute-done.8
  248.1 274.0 %all-reduce.8.cloned.1.call-done = (f32[221184]{0:T(1024)}, f32[442368]{0:T(1024)}, f32[65536]{0:T(1024)}) async-done(((f32[221184]{0:T(1024)}, f32[442368]{0:T(1024)}, f32[65536]{0:T(1024)}), (f32[221184]{0:T(1024)}, f32[442368]{0:T(1024)}, f32[65536]{0:T(1024)})) %all-reduce.8.cloned.1.call-update) | async-done | bytes 2916368 | tf_op jit(solution)/shard_map/psum | solution.py:348
  524.1 81.0 %all-reduce.10.cloned.1.call-done = (f32[221184]{0:T(1024)}, f32[442368]{0:T(1024)}, f32[65536]{0:T(1024)}) async-done(((f32[221184]{0:T(1024)}, f32[442368]{0:T(1024)}, f32[65536]{0:T(1024)}), (f32[221184]{0:T(1024)}, f32[442368]{0:T(1024)}, f32[65536]{0:T(1024)})) %all-reduce.10.cloned.1.call-update) | async-done | bytes 2916368 | tf_op jit(solution)/shard_map/psum | solution.py:348
  (638 shorter events, 159.6 us)
Async XLA Ops:
  7.2 514.9 %all-reduce.8.cloned.1.call-start = ((), (), s32[]{:S(2)}) async-start(), calls=%async_computation | async-start | bytes 5832704 | tf_op jit(solution)/shard_map/psum | solution.py:348
  10.0 15.2 %collective-permute-start = (bf16[24,3,4,256]{3,0,2,1:T(8,128)(2,1)S(1)}, bf16[24,3,4,256]{3,0,2,1:T(8,128)(2,1)S(1)}, u32[]{:S(2)}, u32[]{:S(2)}) collective-permute-start(bf16[24,3,4,256]{3,0,2,1:T(8,128)(2,1)S(1)} %constant_dynamic-update-slice_fusion), channel_id=1, source_target_pairs={{0,1},{1,2},{2,3},{3,4},{4,5},{5,6},{6,7},{7,8},{8,9},{9,10},{10,1... | collective-permute-start | bytes 442376 | tf_op jit(solution)/shard_map/ppermute | solution.py:23
  15.0 76.9 %copy-start.45 = (s32[1024]{0:T(1024)}, s32[1024]{0:T(1024)S(1)}, u32[]{:S(2)}) copy-start(s32[1024]{0:T(1024)S(1)} %get-tuple-element.874) | copy-start | bytes 12292
  15.0 77.6 %copy-start.48 = (s32[1024]{0:T(1024)}, s32[1024]{0:T(1024)S(1)}, u32[]{:S(2)}) copy-start(s32[1024]{0:T(1024)S(1)} %get-tuple-element.873) | copy-start | bytes 12292
  15.0 78.3 %copy-start.47 = (s32[1024]{0:T(1024)}, s32[1024]{0:T(1024)S(1)}, u32[]{:S(2)}) copy-start(s32[1024]{0:T(1024)S(1)} %get-tuple-element.872) | copy-start | bytes 12292
  15.1 79.1 %copy-start.50 = (s32[1024]{0:T(1024)}, s32[1024]{0:T(1024)S(1)}, u32[]{:S(2)}) copy-start(s32[1024]{0:T(1024)S(1)} %get-tuple-element.871) | copy-start | bytes 12292
  15.1 79.8 %copy-start.49 = (s32[1024]{0:T(1024)}, s32[1024]{0:T(1024)S(1)}, u32[]{:S(2)}) copy-start(s32[1024]{0:T(1024)S(1)} %get-tuple-element.870) | copy-start | bytes 12292
  15.1 80.6 %copy-start.52 = (s32[1024]{0:T(1024)}, s32[1024]{0:T(1024)S(1)}, u32[]{:S(2)}) copy-start(s32[1024]{0:T(1024)S(1)} %get-tuple-element.869) | copy-start | bytes 12292
  15.1 81.3 %copy-start.51 = (s32[1024]{0:T(1024)}, s32[1024]{0:T(1024)S(1)}, u32[]{:S(2)}) copy-start(s32[1024]{0:T(1024)S(1)} %get-tuple-element.868) | copy-start | bytes 12292
  15.1 82.0 %copy-start.54 = (s32[1024]{0:T(1024)}, s32[1024]{0:T(1024)S(1)}, u32[]{:S(2)}) copy-start(s32[1024]{0:T(1024)S(1)} %get-tuple-element.867) | copy-start | bytes 12292
  15.1 82.7 %copy-start.53 = (s32[1024]{0:T(1024)}, s32[1024]{0:T(1024)S(1)}, u32[]{:S(2)}) copy-start(s32[1024]{0:T(1024)S(1)} %get-tuple-element.866) | copy-start | bytes 12292
  15.2 83.4 %copy-start.56 = (s32[1024]{0:T(1024)}, s32[1024]{0:T(1024)S(1)}, u32[]{:S(2)}) copy-start(s32[1024]{0:T(1024)S(1)} %get-tuple-element.865) | copy-start | bytes 12292
  15.2 84.1 %copy-start.55 = (s32[1024]{0:T(1024)}, s32[1024]{0:T(1024)S(1)}, u32[]{:S(2)}) copy-start(s32[1024]{0:T(1024)S(1)} %get-tuple-element.864) | copy-start | bytes 12292
  15.8 84.3 %copy-start.58 = (s32[1024]{0:T(1024)}, s32[1024]{0:T(1024)S(1)}, u32[]{:S(2)}) copy-start(s32[1024]{0:T(1024)S(1)} %get-tuple-element.863) | copy-start | bytes 12292
  15.8 85.0 %copy-start.57 = (s32[1024]{0:T(1024)}, s32[1024]{0:T(1024)S(1)}, u32[]{:S(2)}) copy-start(s32[1024]{0:T(1024)S(1)} %get-tuple-element.862) | copy-start | bytes 12292
  62.0 5.5 collective-permute-start.1
  69.1 8.4 %collective-permute-start.3 = (bf16[6,6,4,512]{3,2,0,1:T(4,128)(2,1)S(1)}, bf16[6,6,4,512]{3,2,0,1:T(4,128)(2,1)S(1)}, u32[]{:S(2)}, u32[]{:S(2)}) collective-permute-start(bf16[6,6,4,512]{3,2,0,1:T(4,128)(2,1)S(1)} %constant_dynamic-update-slice_fusion.30), channel_id=1, source_target_pairs={{1,0},{2,1},{3,2},{4,3},{5,4},{6,5},{7,6},{8,7},{9,8},{10,9},{11,1... | collective-permute-start | bytes 442376 | tf_op jit(solution)/shard_map/ppermute | solution.py:15
  74.8 9.1 %collective-permute-start.2 = (bf16[6,6,4,512]{3,2,0,1:T(4,128)(2,1)S(1)}, bf16[6,6,4,512]{3,2,0,1:T(4,128)(2,1)S(1)}, u32[]{:S(2)}, u32[]{:S(2)}) collective-permute-start(bf16[6,6,4,512]{3,2,0,1:T(4,128)(2,1)S(1)} %constant_dynamic-update-slice_fusion.30), channel_id=1, source_target_pairs={{0,1},{1,2},{2,3},{3,4},{4,5},{5,6},{6,7},{7,8},{8,9},{9,10},{10,1... | collective-permute-start | bytes 442376 | tf_op jit(solution)/shard_map/ppermute | solution.py:14
  123.6 15.2 %collective-permute-start.4 = (bf16[8,2,2,256]{3,0,2,1:T(8,128)(2,1)S(1)}, bf16[8,2,2,256]{3,0,2,1:T(8,128)(2,1)S(1)}, u32[]{:S(2)}, u32[]{:S(2)}) collective-permute-start(bf16[8,2,2,256]{3,0,2,1:T(8,128)(2,1)S(1)} %bitcast.517), channel_id=1, source_target_pairs={{0,1},{1,2},{2,3},{3,4},{4,5},{5,6},{6,7},{7,8},{8,9},{9,10},{10,1... | collective-permute-start | bytes 49160 | tf_op jit(solution)/shard_map/ppermute | solution.py:23
  142.6 7.5 %collective-permute-start.5 = (bf16[1,2,2,256]{3,2,1,0:T(2,128)(2,1)S(1)}, bf16[1,2,2,256]{3,2,1,0:T(2,128)(2,1)S(1)}, u32[]{:S(2)}, u32[]{:S(2)}) collective-permute-start(bf16[1,2,2,256]{3,2,1,0:T(2,128)(2,1)S(1)} %slice.3357), channel_id=1, source_target_pairs={{1,0},{2,1},{3,2},{4,3},{5,4},{6,5},{7,6},{8,7},{9,8},{10,9},{11,1... | collective-permute-start | bytes 6152 | tf_op jit(solution)/shard_map/ppermute | solution.py:23
  152.0 11.8 %collective-permute-start.7 = (bf16[6,6,4,512]{3,2,0,1:T(4,128)(2,1)S(1)}, bf16[6,6,4,512]{3,2,0,1:T(4,128)(2,1)S(1)}, u32[]{:S(2)}, u32[]{:S(2)}) collective-permute-start(bf16[6,6,4,512]{3,2,0,1:T(4,128)(2,1)S(1)} %constant_dynamic-update-slice_fusion.36), channel_id=1, source_target_pairs={{1,0},{2,1},{3,2},{4,3},{5,4},{6,5},{7,6},{8,7},{9,8},{10,9},{11,1... | collective-permute-start | bytes 442376 | tf_op jit(solution)/shard_map/ppermute | solution.py:15
  158.3 9.1 %collective-permute-start.6 = (bf16[6,6,4,512]{3,2,0,1:T(4,128)(2,1)S(1)}, bf16[6,6,4,512]{3,2,0,1:T(4,128)(2,1)S(1)}, u32[]{:S(2)}, u32[]{:S(2)}) collective-permute-start(bf16[6,6,4,512]{3,2,0,1:T(4,128)(2,1)S(1)} %constant_dynamic-update-slice_fusion.36), channel_id=1, source_target_pairs={{0,1},{1,2},{2,3},{3,4},{4,5},{5,6},{6,7},{7,8},{8,9},{9,10},{10,1... | collective-permute-start | bytes 442376 | tf_op jit(solution)/shard_map/ppermute | solution.py:14
  238.0 7.7 %collective-permute-start.8 = (bf16[8,2,2,256]{3,0,2,1:T(8,128)(2,1)S(1)}, bf16[8,2,2,256]{3,0,2,1:T(8,128)(2,1)S(1)}, u32[]{:S(2)}, u32[]{:S(2)}) collective-permute-start(bf16[8,2,2,256]{3,0,2,1:T(8,128)(2,1)S(1)} %bitcast.518), channel_id=1, source_target_pairs={{0,1},{1,2},{2,3},{3,4},{4,5},{5,6},{6,7},{7,8},{8,9},{9,10},{10,1... | collective-permute-start | bytes 49160 | tf_op jit(solution)/shard_map/ppermute | solution.py:23
  248.0 357.1 %all-reduce.10.cloned.1.call-start = ((), (), s32[]{:S(2)}) async-start(), calls=%async_computation.1 | async-start | bytes 5832704 | tf_op jit(solution)/shard_map/psum | solution.py:348
  (59 other events, 920.9 us)
Sparse Core Ops, SparseCore 0:
  248.1 273.8 all-reduce.7
  524.8 80.2 all-reduce.9
